TPU v7x, 1024 devices: a whole 4x8x16 slice. The times are simulated.
1024 devices in a mesh: dp: 32 (over x, y_hi, core), tensor: 32 (over z, y_lo).
Axes of the slice: x: 4, y: 8 (y_hi: 4, y_lo: 2; y = y_hi * 2 + y_lo), z: 16, core: 2. Of those that a mesh axis runs over, the one named last changes fastest.
Arguments:
- latent_with_rope: bfloat16 [16384, 576], P('dp'), may hold values from -120 to 120
- latent_norm_weight: float32 [512], replicated, may hold values from 0.1 to 1.9
- expand_weight: bfloat16 [512, 32768], P(None, 'tensor'), may hold values from -0.25 to 0.25
- queries: bfloat16 [16384, 24576], P('dp', 'tensor'), may hold values from -64 to 64
- grad_output: bfloat16 [16384, 16384], P('dp', 'tensor'), may hold values from -24 to 24
Outputs:
- grad_queries: bfloat16 [16384, 24576], P('dp', 'tensor')
- grad_joint_latent: bfloat16 [16384, 576], P('dp')
- grad_up_weight: float32 [512, 32768], P('dp', 'tensor')
- grad_gain: float32 [512], replicated
All inputs are finite; a program needn't handle non-finite values.
Results may differ from a plain program's by a relative error of at most 0.034.
Values may be sent and summed in bfloat16 or wider, within the bound.
A program may use at most 32 MiB of HBM per device.

v0:
```python
import math

import jax
import jax.numpy as jnp
from jax import lax
from jax.sharding import PartitionSpec as P

ROPE = 64
PLAIN_HEAD_DIM = 128
VALUE_HEAD_DIM = 128


soft_scale = (1.0 + 0.1 * math.log(40.0)) ** 2 / math.sqrt(192.0)
epsilon = 1e-06


def head_backward(query_h, grad_h, key_nope, rotated_key_part, value):
    key_full = jnp.concatenate([key_nope, rotated_key_part], axis=1)
    seq_len = query_h.shape[0]
    scores = soft_scale * jnp.dot(query_h, key_full.T, preferred_element_type=jnp.float32)
    row_index = lax.broadcasted_iota(jnp.int32, (seq_len, seq_len), 0)
    col_index = lax.broadcasted_iota(jnp.int32, (seq_len, seq_len), 1)
    scores = jnp.where(col_index <= row_index, scores, -jnp.inf)
    row_max = jnp.max(scores, axis=1, keepdims=True)
    weights = jnp.exp(scores - row_max)
    probs = weights / jnp.sum(weights, axis=1, keepdims=True)
    prob_low = probs.astype(jnp.bfloat16)
    grad_value = jnp.dot(prob_low.T, grad_h, preferred_element_type=jnp.float32)
    grad_probs = jnp.dot(grad_h, value.T, preferred_element_type=jnp.float32)
    row_delta = jnp.sum(probs * grad_probs, axis=1, keepdims=True)
    grad_scores = (soft_scale * probs * (grad_probs - row_delta)).astype(jnp.bfloat16)
    grad_query = jnp.dot(grad_scores, key_full, preferred_element_type=jnp.float32).astype(
        jnp.bfloat16
    )
    grad_key = jnp.dot(grad_scores.T, query_h, preferred_element_type=jnp.float32)
    grad_up_h = jnp.concatenate([grad_key[:, :PLAIN_HEAD_DIM], grad_value], axis=1).astype(
        jnp.bfloat16
    )
    return (grad_query, grad_up_h, grad_key[:, PLAIN_HEAD_DIM:])


def norm_backward(grad_normed, unit, inverse, latent_norm_weight):
    scaled = grad_normed * latent_norm_weight
    return inverse * (scaled - unit * jnp.mean(scaled * unit, axis=1, keepdims=True))


def per_device(latent_with_rope, latent_norm_weight, expand_weight, queries, grad_output):
    latent_width = expand_weight.shape[0]
    seq_len = latent_with_rope.shape[0]
    heads_dev = queries.shape[1] // (PLAIN_HEAD_DIM + ROPE)
    latent_state = latent_with_rope[:, :latent_width].astype(jnp.float32)
    rotated_key_part = latent_with_rope[:, latent_width:]
    inverse = lax.rsqrt(jnp.mean(latent_state * latent_state, axis=1, keepdims=True) + epsilon)
    unit = latent_state * inverse
    normed = (unit * latent_norm_weight).astype(jnp.bfloat16)
    projected = jnp.dot(normed, expand_weight, preferred_element_type=jnp.float32).astype(
        jnp.bfloat16
    )

    def one_head(head_operands):
        up_h, query_h, grad_h = head_operands
        return head_backward(
            query_h, grad_h, up_h[:, :PLAIN_HEAD_DIM], rotated_key_part, up_h[:, PLAIN_HEAD_DIM:]
        )

    grad_query, grad_up, grad_rope_h = lax.map(
        one_head,
        (
            projected.reshape(seq_len, heads_dev, PLAIN_HEAD_DIM + VALUE_HEAD_DIM).transpose(
                1, 0, 2
            ),
            queries.reshape(seq_len, heads_dev, PLAIN_HEAD_DIM + ROPE).transpose(1, 0, 2),
            grad_output.reshape(seq_len, heads_dev, VALUE_HEAD_DIM).transpose(1, 0, 2),
        ),
    )
    grad_queries = grad_query.transpose(1, 0, 2).reshape(
        seq_len, heads_dev * (PLAIN_HEAD_DIM + ROPE)
    )
    grad_up = grad_up.transpose(1, 0, 2).reshape(
        seq_len, heads_dev * (PLAIN_HEAD_DIM + VALUE_HEAD_DIM)
    )
    grad_rope = jnp.sum(grad_rope_h, axis=0)
    grad_up_weight = lax.psum_scatter(
        lax.dot_general(
            normed, grad_up, (((0,), (0,)), ((), ())), preferred_element_type=jnp.float32
        ).astype(jnp.bfloat16),
        "dp",
        scatter_dimension=0,
        tiled=True,
    ).astype(jnp.float32)
    grad_normed = lax.dot_general(
        grad_up, expand_weight, (((1,), (1,)), ((), ())), preferred_element_type=jnp.float32
    )
    totals = (
        lax.psum(grad_normed.astype(jnp.bfloat16), "tensor").astype(jnp.float32),
        lax.psum(grad_rope.astype(jnp.bfloat16), "tensor").astype(jnp.float32),
    )
    grad_latent = norm_backward(totals[0], unit, inverse, latent_norm_weight)
    grad_joint_latent = jnp.concatenate([grad_latent, totals[1]], axis=1).astype(jnp.bfloat16)
    grad_gain = lax.psum(jnp.sum(totals[0] * unit, axis=0), "dp")
    return (grad_queries, grad_joint_latent, grad_up_weight, grad_gain)


def solution(mesh):
    placed = (P("dp", None), P(), P(None, "tensor"), P("dp", "tensor"), P("dp", "tensor"))
    return jax.shard_map(
        per_device,
        mesh=mesh,
        in_specs=placed,
        out_specs=(P("dp", "tensor"), P("dp", None), P("dp", "tensor"), P()),
        check_vma=False,
    )
```

profile of v0, /device:TPU:1, one launch (start us, length us, event | category | flops | bytes accessed | tf_op | source)
XLA Modules:
  0.0 398.2 jit_solution(1365113170631927942)
XLA Ops:
  8.1 1.5 copy.33
  10.3 0.8 convolution_convert_fusion.3
  11.2 0.8 slice-done.1
  11.9 0.7 copy.46
  12.7 2.1 copy.37
  14.8 19.2 %while.14 = (s32[]{:T(128)}, bf16[4,512,192]{1,2,0:T(8,128)(2,1)}, bf16[4,512,256]{1,2,0:T(8,128)(2,1)}, f32[4,512,64]{1,2,0:T(8,128)}, bf16[4,512,192]{1,2,0:T(...) while((s32[]{:T(128)}, bf16[4,512,192]{1,2,0:T(8,128)(2,1)}, ...), condition=%wide.region_5.6_spmd, body=%wide.region_1.5_spmd.sunk | while | flops 442661376 | bytes 14833825 | solution.py:66
  14.8 0.3 fusion.63
  15.4 0.5 copy-done.3
  15.9 0.3 multiply_reduce_fusion.2
  16.5 1.0 fusion.65
  17.5 0.3 fusion.66
  17.8 0.3 fusion.67
  18.2 0.7 maximum_dynamic-update-slice_fusion.2
  18.9 0.7 fusion.69
  19.6 0.3 fusion.63
  20.2 0.5 copy-done.3
  20.7 0.3 multiply_reduce_fusion.2
  21.3 1.0 fusion.65
  22.3 0.3 fusion.66
  22.6 0.3 fusion.67
  23.0 0.7 maximum_dynamic-update-slice_fusion.2
  23.7 0.7 fusion.69
  24.4 0.3 fusion.63
  25.0 0.5 copy-done.3
  25.5 0.3 multiply_reduce_fusion.2
  26.1 1.0 fusion.65
  27.1 0.3 fusion.66
  27.4 0.3 fusion.67
  27.8 0.7 maximum_dynamic-update-slice_fusion.2
  28.5 0.7 fusion.69
  29.7 0.5 copy-done.3
  30.9 1.0 fusion.65
  31.9 0.3 fusion.66
  32.2 0.3 fusion.67
  32.6 0.7 maximum_dynamic-update-slice_fusion.2
  33.3 0.7 fusion.69
  34.0 2.8 convolution_convert_fusion.4
  36.8 0.7 reduce_sum.56
  37.6 0.5 copy-done.7
  38.1 1.9 convolution_convert_fusion.2
  40.0 1.1 copy-done.2
  41.1 1.2 copy.41
  42.3 250.6 %all-reduce.3.cloned.1.call-done = (bf16[512,64]{0,1:T(8,128)(2,1)}, bf16[512,512]{1,0:T(8,128)(2,1)}) async-done(((bf16[512,64]{0,1:T(8,128)(2,1)}, bf16[512,512]{1,0:T(8,128)(2,1)}), (bf16[512,64]{0,1:T(8,128)(2,1)}, bf16[512,512]{1,0:T(8,128)(2,1)})) %all-reduce.3.cloned.1.call-update) | async-done | bytes 589840 | tf_op jit(solution)/shard_map/psum | solution.py:96
  292.8 1.0 copy.40
  293.9 1.5 fusion.36
  295.8 1.1 copy.42
  296.8 92.6 %psum.23 = f32[512]{0:T(512)} all-reduce(f32[512]{0:T(512)S(1)} %get-tuple-element.91), channel_id=1, replica_groups=mesh['dp'=32,'tensor'=32] {'dp'}, use_global_device_ids=true, to_apply=%region_12.13 | all-reduce | flops 512 | bytes 4096 | tf_op jit(solution)/shard_map/psum | solution.py:100
  389.4 1.4 convert_element_type.50
  (56 shorter events, 4.0 us)
Async XLA Ops:
  8.0 2.0 copy-start
  8.0 284.8 %all-reduce.3.cloned.1.call-start = ((), (), s32[]{:S(2)}) async-start(), calls=%async_computation.2 | async-start | bytes 1179648 | tf_op jit(solution)/shard_map/psum | solution.py:96
  8.1 1.5 slice-start
  9.6 0.7 copy-start.6
  11.1 0.8 slice-start.1
  12.7 2.1 copy-start.5
  14.8 1.0 copy-start.3
  19.6 1.0 copy-start.3
  24.4 1.0 copy-start.3
  29.2 1.0 copy-start.3
  34.0 2.9 copy-start.4
  36.8 1.2 copy-start.7
  37.5 351.9 %reduce-scatter.2.cloned.1.call-start = ((), (), s32[]{:S(2)}) async-start(), calls=%async_computation.1 | async-start | bytes 1081344 | tf_op jit(solution)/shard_map/reduce_scatter | solution.py:83
  40.0 1.1 copy-start.2
  292.8 2.6 copy-start.1
Sparse Core Ops, SparseCore 0:
  37.6 255.1 all-reduce.2
Sparse Core Ops, SparseCore 1:
  44.4 120.1 reduce-scatter.1
where the time goes:
time: 399 us; the launch traced here: 398 us
  waiting for transfers between devices  251 us (63%)
  blocking collectives  92.6 us (23%)
  between operations  15.6 us (4%)
  local copies, waits for them, and re-layouts  15.4 us (4%)
  matrix products  14.8 us (4%)
  other arithmetic  8.99 us (2%)
    psum x1, waiting for transfers between devices, per_device(): lax.psum(grad_rope.astype(jnp.bfloat16), 'tensor').astype(jnp.float32)  251 us
    psum x1, blocking collectives, per_device(): grad_gain = lax.psum(jnp.sum(totals[0] * unit, axis=0), 'dp')  92.6 us
    unnamed x20, local copies, waits for them, and re-layouts  8.68 us
  transfers between devices with their start and end apart: 2, of which 1 were waited for; matrix products, arithmetic and copies ran while one was open for 2% of the time, Pallas kernels for 0%

commit v1 on v0

v1 whole, which is shorter than its diff:
```python
import functools
import math

import jax
import jax.numpy as jnp
from jax import lax
from jax.experimental import pallas as pl
from jax.experimental.pallas import tpu as pltpu
from jax.sharding import PartitionSpec as P

ROPE = 64
NOPE = 128
VALUE = 128
LATENT = 512
JOINT = LATENT + ROPE
SEQ = 512
HALF = SEQ // 2
CHUNK = 16
NX, NY, NCORE = 4, 4, 2
NZ, NLO = 16, 2

soft_scale = (1.0 + 0.1 * math.log(40.0)) ** 2 / math.sqrt(192.0)
exp2_scale = soft_scale * math.log2(math.e)
epsilon = 1e-06

F32 = jnp.float32
BF16 = jnp.bfloat16
MESH = pl.DeviceIdType.MESH


def dot(a, b, contract):
    return lax.dot_general(a, b, (contract, ((), ())), preferred_element_type=F32)


def head_probs(scores, grads):
    keep = lax.broadcasted_iota(jnp.int32, (HALF, HALF), 0) <= lax.broadcasted_iota(
        jnp.int32, (HALF, HALF), 1
    )
    scores = scores[:-1] + [jnp.where(keep, scores[-1], -jnp.inf)]
    top = functools.reduce(
        jnp.maximum, [jnp.max(block, axis=0, keepdims=True) for block in scores]
    )
    shift = top * exp2_scale
    weights = [jnp.exp2(block * exp2_scale - shift) for block in scores]
    total = sum(jnp.sum(block, axis=0, keepdims=True) for block in weights)
    inverse = 1.0 / total
    probs = [block * inverse for block in weights]
    delta = sum(
        jnp.sum(prob * grad, axis=0, keepdims=True) for prob, grad in zip(probs, grads)
    )
    grad_scores = [
        (prob * (grad - delta) * soft_scale).astype(BF16) for prob, grad in zip(probs, grads)
    ]
    return [prob.astype(BF16) for prob in probs], grad_scores


def compute_body(lat, weight, expand, query, grad_out, grad_query, joint_part, gain_part,
                 up_part, unit, normed, normed_t, rope_pad, rope_sum, grad_up, key_pad, value,
                 probs, grad_scores):
    heads = expand.shape[1] // (NOPE + VALUE)
    state = lat[:, :LATENT].astype(F32)
    inverse = lax.rsqrt(jnp.mean(state * state, axis=1, keepdims=True) + epsilon)
    unit[...] = state * inverse
    scaled = unit[...] * weight[...]
    normed[...] = scaled.astype(BF16)
    normed_t[...] = scaled.T.astype(BF16)
    rope_pad[...] = jnp.zeros_like(rope_pad)
    rope_pad[:, :ROPE] = lat[:, LATENT:].astype(F32)
    rope_sum[...] = jnp.zeros_like(rope_sum)

    low, high, whole = slice(0, HALF), slice(HALF, SEQ), slice(0, SEQ)
    for head in range(heads):
        odd = head % 2
        columns = slice(head * 256, (head + 1) * 256)
        wide = slice((head // 2) * 384 + odd * 128, (head // 2) * 384 + odd * 128 + 256)
        own = slice(head * VALUE, (head + 1) * VALUE)
        projected = dot(normed[...], expand[:, columns], ((1,), (0,)))
        value[...] = projected[:, NOPE:].astype(BF16)
        keys = jnp.concatenate([projected[:, :NOPE], rope_pad[...]], axis=1)
        if odd:
            keys = pltpu.roll(keys, 64, 1)
        key_pad[...] = keys.astype(BF16)
        for rows, blocks in ((low, (low,)), (high, (low, high))):
            scores = [dot(key_pad[b, :], query[rows, wide], ((1,), (1,))) for b in blocks]
            grads = [dot(value[b, :], grad_out[rows, own], ((1,), (1,))) for b in blocks]
            prob, grad_score = head_probs(scores, grads)
            for b, p, g in zip(blocks, prob, grad_score):
                probs[b, rows] = p
                grad_scores[b, rows] = g
        out_low = dot(grad_scores[low, low], key_pad[low, :], ((0,), (0,)))
        out_high = dot(grad_scores[:, high], key_pad[...], ((0,), (0,)))
        base = (head // 2) * 384
        for rows, out in ((low, out_low), (high, out_high)):
            if odd:
                grad_query[rows, base + 128:base + 256] = (
                    grad_query[rows, base + 128:base + 256] + out[:, :128].astype(BF16)
                )
                grad_query[rows, base + 256:base + 384] = out[:, 128:].astype(BF16)
            else:
                grad_query[rows, base:base + 256] = out.astype(BF16)
        for rows, used in ((low, whole), (high, high)):
            grad_key = dot(grad_scores[rows, used], query[used, wide], ((1,), (0,)))
            grad_value = dot(probs[rows, used], grad_out[used, own], ((1,), (0,)))
            if odd:
                grad_key = pltpu.roll(grad_key, 192, 1)
            grad_up[rows, head * 256:head * 256 + NOPE] = grad_key[:, :NOPE].astype(BF16)
            grad_up[rows, head * 256 + NOPE:(head + 1) * 256] = grad_value.astype(BF16)
            rope_sum[rows, :] += grad_key[:, NOPE:]

    gain = jnp.zeros((1, LATENT), F32)
    for quarter in range(4):
        rows = slice(quarter * 128, (quarter + 1) * 128)
        grad_normed = dot(grad_up[rows, :], expand[...], ((1,), (1,)))
        gain = gain + jnp.sum(grad_normed * unit[rows, :], axis=0, keepdims=True)
        joint_part[quarter, :, :, :, :LATENT] = grad_normed.astype(BF16).reshape(
            2, 4, CHUNK, LATENT
        )
        joint_part[quarter, :, :, :, LATENT:] = rope_sum[rows, :ROPE].astype(BF16).reshape(
            2, 4, CHUNK, ROPE
        )
    gain_part[...] = jnp.zeros_like(gain_part)
    for piece in range(4):
        gain_part[piece:piece + 1, :] = gain[:, piece * 128:(piece + 1) * 128]
    for head in range(heads):
        columns = slice(head * 256, (head + 1) * 256)
        up_part[:, :, :, columns] = (
            dot(normed_t[...], grad_up[:, columns], ((1,), (0,)))
            .astype(BF16)
            .reshape(16, 2, CHUNK, 256)
        )


def comm_body(lat, weight, joint_part, gain_part, up_part, joint, up, gain_out,
              lo_in, lo_sum, near_in, near_sum, far_in, core_in, core_sum, x_in, y_sum, y_in,
              gain_lo, gain_core, gain_far, gain_near, gain_x, gain_y,
              lo_sem, near_sem, far_sem, core_sem, x_sem, y_sem, out_far_sem, out_near_sem,
              out_lo_sem, gain_pair_sem, gain_quad_sem):
    d, t = lax.axis_index("dp"), lax.axis_index("tensor")
    core, y, x = d % 2, (d // 2) % 4, d // 8
    lo, z = t % 2, t // 2
    quarter, phase = z // 4, z % 4

    def at_z(other):
        return (d, other * 2 + lo)

    def z_plus(step):
        return at_z((z + (step + NZ)) % NZ)

    lo_peer = (d, t + 1 - 2 * lo)
    core_peer = (d + 1 - 2 * core, t)
    x_peers = [((((x + j) % 4) * 4 + y) * 2 + core, t) for j in (1, 2, 3)]
    y_peers = [((x * 4 + (y + j) % 4) * 2 + core, t) for j in (1, 2, 3)]
    far_peers = [z_plus(4 * j) for j in (1, 2, 3)]
    near_peers = {s: z_plus(s) for s in (1, -1, 2, -2)}

    barrier = pltpu.get_barrier_semaphore()
    peers = [lo_peer, core_peer] + x_peers + y_peers + far_peers + list(near_peers.values())
    for peer in peers:
        pl.semaphore_signal(barrier, inc=1, device_id=peer, device_id_type=MESH)
    pl.semaphore_wait(barrier, len(peers))

    started = []

    def send(src, dst, sems, slot, recv_slot, peer):
        copy = pltpu.make_async_remote_copy(
            src_ref=src, dst_ref=dst, send_sem=sems.at[(0,) + slot],
            recv_sem=sems.at[(1,) + recv_slot], device_id=peer, device_id_type=MESH,
        )
        copy.start()
        started.append(copy)

    def arrive(dst, sems, recv_slot, peer):
        pltpu.make_async_remote_copy(
            src_ref=dst, dst_ref=dst, send_sem=sems.at[(0,) + recv_slot],
            recv_sem=sems.at[(1,) + recv_slot], device_id=peer, device_id_type=MESH,
        ).wait_recv()

    def gain_pair_send(value, slots, index, me, peer):
        slots[me] = value
        send(slots.at[me], slots.at[me], gain_pair_sem, (index,), (index,), peer)

    def gain_pair_sum(slots, index, me, peer):
        arrive(slots.at[1 - me], gain_pair_sem, (index,), peer)
        return slots[0] + slots[1]

    def gain_quad_send(value, slots, index, me, peers_of):
        slots[me] = value
        for j, peer in enumerate(peers_of):
            send(slots.at[me], slots.at[me], gain_quad_sem, (index, j), (index, j), peer)

    def gain_quad_sum(slots, index, me, steps, peers_of):
        for j, (step, peer) in enumerate(zip(steps, peers_of)):
            arrive(slots.at[(me + (4 - step)) % 4], gain_quad_sem, (index, j), peer)
        return (slots[0] + slots[1]) + (slots[2] + slots[3])

    for a in range(4):
        send(joint_part.at[a, 1 - lo], lo_in.at[a], lo_sem, (a,), (a,), lo_peer)
    gain_pair_send(gain_part[...], gain_lo, 0, lo, lo_peer)
    for i in range(4):
        send(up_part.at[pl.ds(4 * i, 4), 1 - core], core_in.at[pl.ds(4 * i, 4)], core_sem,
             (i,), (i,), core_peer)

    for a in range(4):
        arrive(lo_in.at[a], lo_sem, (a,), lo_peer)
        lo_sum[a] = (joint_part[a, lo].astype(F32) + lo_in[a].astype(F32)).astype(BF16)
        for i, step in enumerate((1, -1, 2 if a < 2 else -2)):
            other = (phase + (step + 4)) % 4
            send(lo_sum.at[a, other], near_in.at[i, a], near_sem, (i, a), (i, a),
                 near_peers[step])
    gain_value = gain_pair_sum(gain_lo, 0, lo, lo_peer)
    gain_pair_send(gain_value, gain_core, 1, core, core_peer)

    for i in range(4):
        arrive(core_in.at[pl.ds(4 * i, 4)], core_sem, (i,), core_peer)
    for j in (1, 2, 3, 0):
        rows = pl.ds(((x + j) % 4) * 4, 4)
        core_sum[rows] = (
            up_part[rows, core].astype(F32) + core_in[rows].astype(F32)
        ).astype(BF16)
        if j:
            send(core_sum.at[rows], x_in.at[j - 1], x_sem, (j - 1,), (j - 1,), x_peers[j - 1])

    for a in range(4):
        for i, step in enumerate((1, -1, 2 if a < 2 else -2)):
            arrive(near_in.at[i, a], near_sem, (i, a), near_peers[-step])
        near_sum[a] = (
            (lo_sum[a, phase].astype(F32) + near_in[0, a].astype(F32))
            + (near_in[1, a].astype(F32) + near_in[2, a].astype(F32))
        ).astype(BF16)
    for j in (1, 2, 3):
        send(near_sum.at[(quarter + j) % 4], far_in.at[j - 1], far_sem, (j - 1,), (j - 1,),
             far_peers[j - 1])
    gain_value = gain_pair_sum(gain_core, 1, core, core_peer)
    gain_quad_send(gain_value, gain_far, 0, quarter, far_peers)

    for j in (1, 2, 3):
        arrive(x_in.at[j - 1], x_sem, (j - 1,), x_peers[3 - j])
    y_sum[...] = (
        (core_sum[pl.ds(x * 4, 4)].astype(F32) + x_in[0].astype(F32))
        + (x_in[1].astype(F32) + x_in[2].astype(F32))
    ).astype(BF16)
    for j in (1, 2, 3):
        send(y_sum.at[(y + j) % 4], y_in.at[j - 1], y_sem, (j - 1,), (j - 1,), y_peers[j - 1])

    first = pl.multiple_of(quarter * 128 + lo * 64 + phase * CHUNK, CHUNK)
    state = lat[pl.ds(first, CHUNK), :LATENT].astype(F32)
    inverse = lax.rsqrt(jnp.mean(state * state, axis=1, keepdims=True) + epsilon)
    unit = state * inverse
    for j in (1, 2, 3):
        arrive(far_in.at[j - 1], far_sem, (j - 1,), far_peers[3 - j])
    total = (near_sum[quarter].astype(F32) + far_in[0].astype(F32)) + (
        far_in[1].astype(F32) + far_in[2].astype(F32)
    )
    scaled = total[:, :LATENT] * weight[...]
    grad_latent = inverse * (scaled - unit * jnp.mean(scaled * unit, axis=1, keepdims=True))
    joint[quarter, lo, phase, :, :LATENT] = grad_latent.astype(BF16)
    joint[quarter, lo, phase, :, LATENT:] = total[:, LATENT:].astype(BF16)
    for j in (1, 2, 3):
        mine = joint.at[quarter, lo, phase]
        send(mine, mine, out_far_sem, (j - 1,), (j - 1,), far_peers[j - 1])
    gain_value = gain_quad_sum(gain_far, 0, quarter, (1, 2, 3), far_peers[::-1])
    gain_near_peers = [near_peers[1], near_peers[-1], near_peers[2]]
    gain_quad_send(gain_value, gain_near, 1, phase, gain_near_peers)

    for j in (1, 2, 3):
        arrive(y_in.at[j - 1], y_sem, (j - 1,), y_peers[3 - j])
    up[...] = (y_sum[y].astype(F32) + y_in[0].astype(F32)) + (
        y_in[1].astype(F32) + y_in[2].astype(F32)
    )

    for j in (1, 2, 3):
        theirs = joint.at[(quarter + (4 - j)) % 4, lo, phase]
        arrive(theirs, out_far_sem, (j - 1,), far_peers[3 - j])
    for i, step in enumerate((1, -1)):
        mine = joint.at[:, lo, phase]
        send(mine, mine, out_near_sem, (i,), (i,), near_peers[step])
    for i, step in enumerate((2, -2)):
        mine = joint.at[pl.ds(2 * i, 2), lo, phase]
        send(mine, mine, out_near_sem, (2 + i,), (2 + i,), near_peers[step])
    mine = joint.at[:, lo, phase]
    send(mine, mine, out_lo_sem, (0,), (0,), lo_peer)
    gain_value = gain_quad_sum(
        gain_near, 1, phase, (1, 3, 2), [near_peers[-1], near_peers[1], near_peers[-2]]
    )
    gain_quad_send(gain_value, gain_x, 2, x, x_peers)

    for i, step in enumerate((1, -1, 2)):
        other = (phase + (4 - step)) % 4
        theirs = joint.at[:, lo, other]
        if i < 2:
            arrive(theirs, out_near_sem, (i,), near_peers[-step])
        else:
            arrive(joint.at[pl.ds(0, 2), lo, other], out_near_sem, (2,), near_peers[-2])
            arrive(joint.at[pl.ds(2, 2), lo, other], out_near_sem, (3,), near_peers[2])
        send(theirs, theirs, out_lo_sem, (1 + i,), (1 + i,), lo_peer)
    gain_value = gain_quad_sum(gain_x, 2, x, (1, 2, 3), x_peers[::-1])
    gain_quad_send(gain_value, gain_y, 3, y, y_peers)
    gain_value = gain_quad_sum(gain_y, 3, y, (1, 2, 3), y_peers[::-1])
    for piece in range(4):
        gain_out[:, piece * 128:(piece + 1) * 128] = gain_value[piece:piece + 1, :]

    arrive(joint.at[:, 1 - lo, phase], out_lo_sem, (0,), lo_peer)
    for i, step in enumerate((1, -1, 2)):
        other = (phase + (4 - step)) % 4
        arrive(joint.at[:, 1 - lo, other], out_lo_sem, (1 + i,), lo_peer)
    for copy in started:
        copy.wait_send()


def vmem_spec():
    return pl.BlockSpec(memory_space=pltpu.VMEM)


def per_device(latent_with_rope, latent_norm_weight, expand_weight, queries, grad_output):
    width = expand_weight.shape[1]
    weight = latent_norm_weight.reshape(1, LATENT)
    joint_shape = (4, 2, 4, CHUNK, JOINT)
    grad_queries, joint_part, gain_part, up_part = pl.pallas_call(
        compute_body,
        name="attention_backward",
        out_shape=(
            jax.ShapeDtypeStruct(queries.shape, BF16),
            jax.ShapeDtypeStruct(joint_shape, BF16),
            jax.ShapeDtypeStruct((8, 128), F32),
            jax.ShapeDtypeStruct((16, 2, CHUNK, width), BF16),
        ),
        in_specs=[vmem_spec()] * 5,
        out_specs=(vmem_spec(),) * 4,
        scratch_shapes=[
            pltpu.VMEM((SEQ, LATENT), F32),
            pltpu.VMEM((SEQ, LATENT), BF16),
            pltpu.VMEM((LATENT, SEQ), BF16),
            pltpu.VMEM((SEQ, 128), F32),
            pltpu.VMEM((SEQ, 128), F32),
            pltpu.VMEM((SEQ, width), BF16),
            pltpu.VMEM((SEQ, 256), BF16),
            pltpu.VMEM((SEQ, VALUE), BF16),
            pltpu.VMEM((SEQ, SEQ), BF16),
            pltpu.VMEM((SEQ, SEQ), BF16),
        ],
        compiler_params=pltpu.CompilerParams(vmem_limit_bytes=32 * 2**20),
    )(latent_with_rope, weight, expand_weight, queries, grad_output)

    sem = pltpu.SemaphoreType.DMA
    joint, up, gain = pl.pallas_call(
        comm_body,
        name="sums",
        out_shape=(
            jax.ShapeDtypeStruct(joint_shape, BF16),
            jax.ShapeDtypeStruct((CHUNK, width), F32),
            jax.ShapeDtypeStruct((1, LATENT), F32),
        ),
        in_specs=[vmem_spec()] * 5,
        out_specs=(vmem_spec(),) * 3,
        scratch_shapes=[
            pltpu.VMEM((4, 4, CHUNK, JOINT), BF16),
            pltpu.VMEM((4, 4, CHUNK, JOINT), BF16),
            pltpu.VMEM((3, 4, CHUNK, JOINT), BF16),
            pltpu.VMEM((4, CHUNK, JOINT), BF16),
            pltpu.VMEM((3, CHUNK, JOINT), BF16),
            pltpu.VMEM((16, CHUNK, width), BF16),
            pltpu.VMEM((16, CHUNK, width), BF16),
            pltpu.VMEM((3, 4, CHUNK, width), BF16),
            pltpu.VMEM((4, CHUNK, width), BF16),
            pltpu.VMEM((3, CHUNK, width), BF16),
            pltpu.VMEM((2, 8, 128), F32),
            pltpu.VMEM((2, 8, 128), F32),
            pltpu.VMEM((4, 8, 128), F32),
            pltpu.VMEM((4, 8, 128), F32),
            pltpu.VMEM((4, 8, 128), F32),
            pltpu.VMEM((4, 8, 128), F32),
            sem((2, 4)),
            sem((2, 3, 4)),
            sem((2, 3)),
            sem((2, 4)),
            sem((2, 3)),
            sem((2, 3)),
            sem((2, 3)),
            sem((2, 4)),
            sem((2, 4)),
            sem((2, 2)),
            sem((2, 4, 3)),
        ],
        compiler_params=pltpu.CompilerParams(
            collective_id=0, has_side_effects=True, vmem_limit_bytes=24 * 2**20
        ),
    )(latent_with_rope, weight, joint_part, gain_part, up_part)
    return (
        grad_queries,
        joint.reshape(SEQ, JOINT),
        up,
        gain.reshape(LATENT),
    )


def solution(mesh):
    assert mesh.shape["dp"] == NX * NY * NCORE and mesh.shape["tensor"] == NZ * NLO
    placed = (P("dp", None), P(), P(None, "tensor"), P("dp", "tensor"), P("dp", "tensor"))
    return jax.shard_map(
        per_device,
        mesh=mesh,
        in_specs=placed,
        out_specs=(P("dp", "tensor"), P("dp", None), P("dp", "tensor"), P()),
        check_vma=False,
    )
```

time: 399 us -> 76.3 us (0.19)
  the two profiles are of different devices: /device:TPU:1 before, /device:TPU:4 now
where the time goes in v1:
time: 76.3 us; the launch traced here: 76.1 us
  Pallas kernels  69.5 us (91%)
  local copies, waits for them, and re-layouts  5.89 us (8%)
    pallas_call x1, Pallas kernels, per_device(): pl.pallas_call(comm_body, name='sums', out_shape=(jax.ShapeDtypeStruct(jo...  62.9 us
    pallas_call x1, Pallas kernels, per_device(): pl.pallas_call(compute_body, name='attention_backward', out_shape=(jax.Sh...  6.55 us
    unnamed x12, local copies, waits for them, and re-layouts  5.89 us

profile of v1, /device:TPU:4, one launch (start us, length us, event | category | flops | bytes accessed | tf_op | source)
XLA Modules:
  0.0 76.1 jit_solution(12135140549705185913)
XLA Ops:
  0.6 0.0 copy-start
  0.6 0.0 copy-start.3
  0.7 1.4 %copy.9.lat = bf16[512,576]{1,0:T(8,128)(2,1)S(1)} copy(bf16[512,576]{0,1:T(8,128)(2,1)} %param.5) | data formatting | bytes 1179648 | tf_op args[0]
  2.1 0.0 copy-done
  2.1 0.0 copy-done.3
  2.1 0.0 copy-start.1
  2.1 1.1 %copy-done.1 = bf16[512,768]{1,0:T(8,128)(2,1)S(1)} copy-done((bf16[512,768]{1,0:T(8,128)(2,1)S(1)}, bf16[512,768]{1,0:T(8,128)(2,1)}, u32[]{:S(2)}) %copy-start.1) | copy-done | bytes 786456
  3.3 0.0 copy-start.2
  3.3 1.0 %copy-done.2 = bf16[512,512]{1,0:T(8,128)(2,1)S(1)} copy-done((bf16[512,512]{1,0:T(8,128)(2,1)S(1)}, bf16[512,512]{1,0:T(8,128)(2,1)}, u32[]{:S(2)}) %copy-start.2) | copy-done | bytes 524312
  4.3 6.5 %attention_backward.1 = (bf16[512,768]{1,0:T(8,128)(2,1)}, bf16[4,2,4,16,576]{4,3,2,1,0:T(8,128)(2,1)S(1)}, f32[8,128]{1,0:T(8,128)S(1)}, bf16[16,2,16,1024]{3,2,1,0:T(8,128)(2,1)S(1)}) custom-call(bf16[512,576]{1,0:T(8,128)(2,1)S(1)} %copy.9.lat, f32[1,512]{1,0:T(1,128)S(1)} %bitcast.4, bf16[512,1024]{1,0:T(8,128)(2,1)S(1)} %copy-done, ...), custom_call_target="tpu_custom_call" | custom-call | tf_op jit(solution)/shard_map/attention_backward/pallas_call | solution.py:318
  10.9 62.9 %sums.1 = (bf16[4,2,4,16,576]{4,3,2,1,0:T(8,128)(2,1)S(1)}, f32[16,1024]{1,0:T(8,128)S(1)}, f32[1,512]{1,0:T(1,128)S(1)}) custom-call(bf16[512,576]{1,0:T(8,128)(2,1)S(1)} %copy.9.lat, f32[1,512]{1,0:T(1,128)S(1)} %bitcast.5, bf16[4,2,4,16,576]{4,3,2,1,0:T(8,128)(2,1)S(1)} %get-tuple-element.12.joint_part, f32[8,128]{1,0:T(8,128)S(1)} %get-tuple-element.13.gain_part, ...), custom_call_target="tpu_custom_call" | custom-call | tf_op jit(solution)/shard_map/sums/pallas_call | solution.py:345
  73.8 1.1 %copy.11 = bf16[512,576]{0,1:T(8,128)(2,1)} copy(bf16[512,576]{1,0:T(8,128)(2,1)S(1)} %bitcast.3) | data formatting | bytes 1179648
  74.8 0.6 copy.14
  75.5 0.6 copy.15
Async XLA Ops:
  0.6 1.5 %copy-start = (bf16[512,1024]{1,0:T(8,128)(2,1)S(1)}, bf16[512,1024]{1,0:T(8,128)(2,1)}, u32[]{:S(2)}) copy-start(bf16[512,1024]{1,0:T(8,128)(2,1)} %expand.1) | copy-start | bytes 3145732
  0.6 1.5 %copy-start.3 = (f32[512]{0:T(512)S(1)}, f32[512]{0:T(512)}, u32[]{:S(2)}) copy-start(f32[512]{0:T(512)} %param.6) | copy-start | bytes 6148
  2.1 1.1 %copy-start.1 = (bf16[512,768]{1,0:T(8,128)(2,1)S(1)}, bf16[512,768]{1,0:T(8,128)(2,1)}, u32[]{:S(2)}) copy-start(bf16[512,768]{1,0:T(8,128)(2,1)} %query.1) | copy-start | bytes 2359300
  3.3 1.0 %copy-start.2 = (bf16[512,512]{1,0:T(8,128)(2,1)S(1)}, bf16[512,512]{1,0:T(8,128)(2,1)}, u32[]{:S(2)}) copy-start(bf16[512,512]{1,0:T(8,128)(2,1)} %grad_out.1) | copy-start | bytes 1572868

commit v2 on v1

v2 whole, which is shorter than its diff:
```python
import functools
import math

import jax
import jax.numpy as jnp
from jax import lax
from jax.experimental import pallas as pl
from jax.experimental.pallas import tpu as pltpu
from jax.sharding import PartitionSpec as P

ROPE = 64
NOPE = 128
VALUE = 128
LATENT = 512
JOINT = LATENT + ROPE
PADDED = LATENT + 128
SEQ = 512
HALF = SEQ // 2
CHUNK = 16
NX, NY, NCORE = 4, 4, 2
NZ, NLO = 16, 2

soft_scale = (1.0 + 0.1 * math.log(40.0)) ** 2 / math.sqrt(192.0)
exp2_scale = soft_scale * math.log2(math.e)
epsilon = 1e-06

F32 = jnp.float32
BF16 = jnp.bfloat16
MESH = pl.DeviceIdType.MESH


def dot(a, b, contract):
    return lax.dot_general(a, b, (contract, ((), ())), preferred_element_type=F32)


def head_probs(scores, grads):
    keep = lax.broadcasted_iota(jnp.int32, (HALF, HALF), 0) <= lax.broadcasted_iota(
        jnp.int32, (HALF, HALF), 1
    )
    scores = scores[:-1] + [jnp.where(keep, scores[-1], -jnp.inf)]
    top = functools.reduce(
        jnp.maximum, [jnp.max(block, axis=0, keepdims=True) for block in scores]
    )
    shift = top * exp2_scale
    weights = [jnp.exp2(block * exp2_scale - shift) for block in scores]
    total = sum(jnp.sum(block, axis=0, keepdims=True) for block in weights)
    inverse = 1.0 / total
    probs = [block * inverse for block in weights]
    delta = sum(
        jnp.sum(prob * grad, axis=0, keepdims=True) for prob, grad in zip(probs, grads)
    )
    grad_scores = [
        (prob * (grad - delta) * soft_scale).astype(BF16) for prob, grad in zip(probs, grads)
    ]
    return [prob.astype(BF16) for prob in probs], grad_scores


def transposed_rows(row):
    return jnp.broadcast_to(row, (128, row.shape[1])).T


def wide_columns(block):
    return jnp.concatenate([block] * (LATENT // 128), axis=1)


def attention_part(lat, weight, expand, query, grad_out, grad_query, joint_part, gain_part,
                   unit, inverse, normed, normed_t, rope_pad, rope_sum, grad_up, key_pad, value,
                   probs, grad_scores, loads):
    heads = expand.shape[1] // (NOPE + VALUE)
    loads[0].wait()
    loads[1].wait()
    state = lat[:LATENT, :].astype(F32)
    inverse_row = lax.rsqrt(jnp.mean(state * state, axis=0, keepdims=True) + epsilon)
    unit_t = state * inverse_row
    inverse[...] = transposed_rows(inverse_row)
    unit[...] = unit_t.T
    normed[...] = (unit[...] * weight[...]).astype(BF16)
    normed_t[...] = (unit_t * wide_columns(transposed_rows(weight[...]))).astype(BF16)
    rope_pad[...] = jnp.concatenate(
        [lat[LATENT:, :].astype(F32), jnp.zeros((128 - ROPE, SEQ), F32)], axis=0
    ).T
    rope_sum[...] = jnp.zeros_like(rope_sum)

    low, high, whole = slice(0, HALF), slice(HALF, SEQ), slice(0, SEQ)
    loads[2].wait()
    for head in range(heads):
        odd = head % 2
        columns = slice(head * 256, (head + 1) * 256)
        wide = slice((head // 2) * 384 + odd * 128, (head // 2) * 384 + odd * 128 + 256)
        own = slice(head * VALUE, (head + 1) * VALUE)
        projected = dot(normed[...], expand[:, columns], ((1,), (0,)))
        value[...] = projected[:, NOPE:].astype(BF16)
        keys = jnp.concatenate([projected[:, :NOPE], rope_pad[...]], axis=1)
        if odd:
            keys = pltpu.roll(keys, 64, 1)
        key_pad[...] = keys.astype(BF16)
        if head == 0:
            loads[3].wait()
            loads[4].wait()
        for rows, blocks in ((low, (low,)), (high, (low, high))):
            scores = [dot(key_pad[b, :], query[rows, wide], ((1,), (1,))) for b in blocks]
            grads = [dot(value[b, :], grad_out[rows, own], ((1,), (1,))) for b in blocks]
            prob, grad_score = head_probs(scores, grads)
            for b, p, g in zip(blocks, prob, grad_score):
                probs[b, rows] = p
                grad_scores[b, rows] = g
        out_low = dot(grad_scores[low, low], key_pad[low, :], ((0,), (0,)))
        out_high = dot(grad_scores[:, high], key_pad[...], ((0,), (0,)))
        base = (head // 2) * 384
        for rows, out in ((low, out_low), (high, out_high)):
            if odd:
                grad_query[rows, base + 128:base + 256] = (
                    grad_query[rows, base + 128:base + 256] + out[:, :128].astype(BF16)
                )
                grad_query[rows, base + 256:base + 384] = out[:, 128:].astype(BF16)
            else:
                grad_query[rows, base:base + 256] = out.astype(BF16)
        for rows, used in ((low, whole), (high, high)):
            grad_key = dot(grad_scores[rows, used], query[used, wide], ((1,), (0,)))
            grad_value = dot(probs[rows, used], grad_out[used, own], ((1,), (0,)))
            if odd:
                grad_key = pltpu.roll(grad_key, 192, 1)
            grad_up[rows, head * 256:head * 256 + NOPE] = grad_key[:, :NOPE].astype(BF16)
            grad_up[rows, head * 256 + NOPE:(head + 1) * 256] = grad_value.astype(BF16)
            rope_sum[rows, :] += grad_key[:, NOPE:]

    gain = jnp.zeros((1, LATENT), F32)
    for part in range(4):
        rows = slice(part * 128, (part + 1) * 128)
        grad_normed = dot(grad_up[rows, :], expand[...], ((1,), (1,)))
        gain = gain + jnp.sum(grad_normed * unit[rows, :], axis=0, keepdims=True)
        joint_part[part, :, :, :, :LATENT] = grad_normed.astype(BF16).reshape(
            2, 4, CHUNK, LATENT
        )
        joint_part[part, :, :, :, LATENT:] = rope_sum[rows, :].astype(BF16).reshape(
            2, 4, CHUNK, 128
        )
    gain_part[...] = jnp.zeros_like(gain_part)
    for piece in range(4):
        gain_part[piece:piece + 1, :] = gain[:, piece * 128:(piece + 1) * 128]


def up_gradient(normed_t, grad_up, up_part):
    for head in range(grad_up.shape[1] // 256):
        columns = slice(head * 256, (head + 1) * 256)
        up_part[:, :, :, columns] = (
            dot(normed_t[...], grad_up[:, columns], ((1,), (0,)))
            .astype(BF16)
            .reshape(16, 2, CHUNK, 256)
        )


def body(lat_hbm, weight_hbm, expand_hbm, query_hbm, grad_out_hbm,
         grad_query_hbm, joint_hbm, up_hbm, gain_hbm,
         lat, weight, expand, query, grad_out, load_sem, grad_query, joint, up, gain_out, save_sem,
         unit, inverse, normed, normed_t, rope_pad, rope_sum, grad_up, key_pad, value, probs,
         grad_scores, joint_part, gain_part, up_part,
         lo_in, lo_sum, near_in, near_sum, far_in, core_in, core_sum, x_in, y_sum, y_in,
         gain_lo, gain_core, gain_far, gain_near, gain_x, gain_y,
         lo_sem, near_sem, far_sem, core_sem, x_sem, y_sem, out_far_sem, out_near_sem,
         out_lo_sem, gain_pair_sem, gain_quad_sem):
    d, t = lax.axis_index("dp"), lax.axis_index("tensor")
    core, y, x = d % 2, (d // 2) % 4, d // 8
    lo, z = t % 2, t // 2
    quarter, phase = z // 4, z % 4

    def z_plus(step):
        return (d, ((z + step + NZ) % NZ) * 2 + lo)

    lo_peer = (d, t + 1 - 2 * lo)
    core_peer = (d + 1 - 2 * core, t)
    x_peers = [((((x + j) % 4) * 4 + y) * 2 + core, t) for j in (1, 2, 3)]
    y_peers = [((x * 4 + (y + j) % 4) * 2 + core, t) for j in (1, 2, 3)]
    far_peers = [z_plus(4 * j) for j in (1, 2, 3)]
    near_peers = {s: z_plus(s) for s in (1, -1, 2, -2)}

    barrier = pltpu.get_barrier_semaphore()
    peers = far_peers + [lo_peer, core_peer] + x_peers + y_peers + list(near_peers.values())
    for peer in peers:
        pl.semaphore_signal(barrier, inc=1, device_id=peer, device_id_type=MESH)

    loads = []
    for i, (src, dst) in enumerate(
        ((lat_hbm, lat), (weight_hbm, weight), (expand_hbm, expand), (query_hbm, query),
         (grad_out_hbm, grad_out))
    ):
        loads.append(pltpu.make_async_copy(src, dst, load_sem.at[i]))
        loads[-1].start()

    attention_part(lat, weight, expand, query, grad_out, grad_query, joint_part, gain_part,
                   unit, inverse, normed, normed_t, rope_pad, rope_sum, grad_up, key_pad, value,
                   probs, grad_scores, loads)
    saves = [pltpu.make_async_copy(grad_query, grad_query_hbm, save_sem.at[0])]
    saves[0].start()

    pl.semaphore_wait(barrier, len(peers))

    started = []

    def send(src, dst, sems, slot, recv_slot, peer):
        copy = pltpu.make_async_remote_copy(
            src_ref=src, dst_ref=dst, send_sem=sems.at[(0,) + slot],
            recv_sem=sems.at[(1,) + recv_slot], device_id=peer, device_id_type=MESH,
        )
        copy.start()
        started.append(copy)

    def arrive(dst, sems, recv_slot, peer):
        pltpu.make_async_remote_copy(
            src_ref=dst, dst_ref=dst, send_sem=sems.at[(0,) + recv_slot],
            recv_sem=sems.at[(1,) + recv_slot], device_id=peer, device_id_type=MESH,
        ).wait_recv()

    def gain_pair_send(value, slots, index, me, peer):
        slots[me] = value
        send(slots.at[me], slots.at[me], gain_pair_sem, (index,), (index,), peer)

    def gain_pair_sum(slots, index, me, peer):
        arrive(slots.at[1 - me], gain_pair_sem, (index,), peer)
        return slots[0] + slots[1]

    def gain_quad_send(value, slots, index, me, peers_of):
        slots[me] = value
        for j, peer in enumerate(peers_of):
            send(slots.at[me], slots.at[me], gain_quad_sem, (index, j), (index, j), peer)

    def gain_quad_sum(slots, index, me, steps, peers_of):
        for j, (step, peer) in enumerate(zip(steps, peers_of)):
            arrive(slots.at[(me + (4 - step)) % 4], gain_quad_sem, (index, j), peer)
        return (slots[0] + slots[1]) + (slots[2] + slots[3])

    order = (2, 1, 3, 0)
    deltas = (0, 1, -1, 2)
    slot_of = {1: 0, -1: 1, 2: 2}

    def collected(step, delta):
        holder = quarter if delta in (0, 2) else ((z + delta + NZ) % NZ) // 4
        return (holder + step) % 4, (phase + delta + 4) % 4

    def two_away(a):
        return 2 - 4 * (a // 2)

    gain_pair_send(gain_part[...], gain_lo, 0, lo, lo_peer)
    for step in order:
        for delta in deltas:
            a, k = collected(step, delta)
            send(joint_part.at[a, 1 - lo, k], lo_in.at[a, k], lo_sem, (a, k), (a, k), lo_peer)

    up_gradient(normed_t, grad_up, up_part)
    for i in range(4):
        send(up_part.at[pl.ds(4 * i, 4), 1 - core], core_in.at[pl.ds(4 * i, 4)], core_sem,
             (i,), (i,), core_peer)

    def lo_step(step):
        for delta in deltas:
            a, k = collected(step, delta)
            arrive(lo_in.at[a, k], lo_sem, (a, k), lo_peer)
            lo_sum[a, k] = (
                joint_part[a, lo, k].astype(F32) + lo_in[a, k].astype(F32)
            ).astype(BF16)
            if delta:
                slot = slot_of[delta]
                peer = z_plus(two_away(a)) if delta == 2 else near_peers[delta]
                send(lo_sum.at[a, k], near_in.at[slot, a], near_sem, (slot, a), (slot, a), peer)

    def near_step(step):
        a = (quarter + step) % 4
        for delta in deltas[1:]:
            slot = slot_of[delta]
            arrive(near_in.at[slot, a], near_sem, (slot, a), near_peers[-delta])
        near_sum[a] = (
            (lo_sum[a, phase].astype(F32) + near_in[0, a].astype(F32))
            + (near_in[1, a].astype(F32) + near_in[2, a].astype(F32))
        ).astype(BF16)
        if step:
            send(near_sum.at[a], far_in.at[step - 1], far_sem, (step - 1,), (step - 1,),
                 far_peers[step - 1])

    lo_step(order[0])
    gain_value = gain_pair_sum(gain_lo, 0, lo, lo_peer)
    gain_pair_send(gain_value, gain_core, 1, core, core_peer)
    lo_step(order[1])
    gain_value = gain_pair_sum(gain_core, 1, core, core_peer)
    gain_quad_send(gain_value, gain_far, 0, quarter, far_peers)

    for i in range(4):
        arrive(core_in.at[pl.ds(4 * i, 4)], core_sem, (i,), core_peer)
    for j in (2, 1, 3, 0):
        rows = pl.ds(((x + j) % 4) * 4, 4)
        core_sum[rows] = (
            up_part[rows, core].astype(F32) + core_in[rows].astype(F32)
        ).astype(BF16)
        if j:
            send(core_sum.at[rows], x_in.at[j - 1], x_sem, (j - 1,), (j - 1,), x_peers[j - 1])

    near_step(order[0])
    lo_step(order[2])
    near_step(order[1])
    lo_step(order[3])
    near_step(order[2])
    near_step(order[3])
    gain_value = gain_quad_sum(gain_far, 0, quarter, (1, 2, 3), far_peers[::-1])
    gain_near_peers = [near_peers[1], near_peers[-1], near_peers[2]]
    gain_quad_send(gain_value, gain_near, 1, phase, gain_near_peers)

    first = pl.multiple_of(quarter * 128 + lo * 64 + phase * CHUNK, CHUNK)
    own_unit = unit[pl.ds(first, CHUNK), :]
    own_inverse = wide_columns(inverse[pl.ds(first, CHUNK), :])
    for j in (1, 3, 2):
        arrive(far_in.at[j - 1], far_sem, (j - 1,), far_peers[3 - j])
    total = (near_sum[quarter].astype(F32) + far_in[0].astype(F32)) + (
        far_in[1].astype(F32) + far_in[2].astype(F32)
    )
    scaled = total[:, :LATENT] * weight[...]
    grad_latent = own_inverse * (
        scaled - own_unit * jnp.mean(scaled * own_unit, axis=1, keepdims=True)
    )
    joint[quarter, lo, phase, :, :LATENT] = grad_latent.astype(BF16)
    joint[quarter, lo, phase, :, LATENT:] = total[:, LATENT:].astype(BF16)

    def to_lo(a, k):
        chunk = joint.at[a, lo, k]
        return pltpu.make_async_remote_copy(
            src_ref=chunk, dst_ref=chunk, send_sem=out_lo_sem.at[0, a, k],
            recv_sem=out_lo_sem.at[1, a, k], device_id=lo_peer, device_id_type=MESH,
        )

    def pass_on(a, k):
        to_lo(a, k).start()

    def spread(step):
        a = (quarter + 4 - step) % 4
        chunk = joint.at[a, lo, phase]
        if step:
            arrive(chunk, out_far_sem, (step - 1,), far_peers[3 - step])
        else:
            for j in (2, 1, 3):
                send(chunk, chunk, out_far_sem, (j - 1,), (j - 1,), far_peers[j - 1])
        for slot, peer in ((2, z_plus(two_away(a))), (0, near_peers[1]), (1, near_peers[-1])):
            send(chunk, chunk, out_near_sem, (slot, a), (slot, a), peer)
        pass_on(a, phase)

    def from_near(step):
        for delta in (1, -1, 2, -2):
            a = (((z - delta + NZ) % NZ) // 4 + 4 - step) % 4
            k = (phase - delta + 4) % 4
            slot = 2 if abs(delta) == 2 else slot_of[delta]

            def relay(a=a, k=k, slot=slot, delta=delta):
                arrive(joint.at[a, lo, k], out_near_sem, (slot, a), near_peers[-delta])
                pass_on(a, k)

            if slot < 2:
                relay()
            else:
                pl.when(a < 2 if delta == 2 else a >= 2)(relay)

    spread(0)
    gain_value = gain_quad_sum(
        gain_near, 1, phase, (1, 3, 2), [near_peers[-1], near_peers[1], near_peers[-2]]
    )
    gain_quad_send(gain_value, gain_x, 2, x, x_peers)
    for j in (1, 3, 2):
        arrive(x_in.at[j - 1], x_sem, (j - 1,), x_peers[3 - j])
    y_sum[...] = (
        (core_sum[pl.ds(x * 4, 4)].astype(F32) + x_in[0].astype(F32))
        + (x_in[1].astype(F32) + x_in[2].astype(F32))
    ).astype(BF16)
    for j in (2, 1, 3):
        send(y_sum.at[(y + j) % 4], y_in.at[j - 1], y_sem, (j - 1,), (j - 1,), y_peers[j - 1])
    from_near(0)
    gain_value = gain_quad_sum(gain_x, 2, x, (1, 2, 3), x_peers[::-1])
    gain_quad_send(gain_value, gain_y, 3, y, y_peers)
    spread(1)
    spread(3)
    from_near(1)
    from_near(3)
    spread(2)
    for j in (1, 3, 2):
        arrive(y_in.at[j - 1], y_sem, (j - 1,), y_peers[3 - j])
    up[...] = (y_sum[y].astype(F32) + y_in[0].astype(F32)) + (
        y_in[1].astype(F32) + y_in[2].astype(F32)
    )
    saves.append(pltpu.make_async_copy(up, up_hbm, save_sem.at[1]))
    saves[-1].start()
    from_near(2)
    gain_value = gain_quad_sum(gain_y, 3, y, (1, 2, 3), y_peers[::-1])
    for piece in range(4):
        gain_out[:, piece * 128:(piece + 1) * 128] = gain_value[piece:piece + 1, :]
    saves.append(pltpu.make_async_copy(gain_out, gain_hbm, save_sem.at[2]))
    saves[-1].start()
    for a in range(4):
        for k in range(4):
            arrive(joint.at[a, 1 - lo, k], out_lo_sem, (a, k), lo_peer)
    saves.append(pltpu.make_async_copy(joint, joint_hbm, save_sem.at[3]))
    saves[-1].start()
    for a in range(4):
        for k in range(4):
            to_lo(a, k).wait_send()
    for copy in started:
        copy.wait_send()
    for save in saves:
        save.wait()


def write_body(grad_query_in, joint_in, up_in, gain_in, grad_query_out, joint_out, up_out, gain_out,
               grad_query, joint, up, gain, joint_t, sems):
    def copies(pairs, first):
        return [
            pltpu.make_async_copy(src, dst, sems.at[first + i]) for i, (src, dst) in enumerate(pairs)
        ]

    reads = copies(
        ((joint_in, joint), (grad_query_in, grad_query), (up_in, up), (gain_in, gain)), 0
    )
    writes = copies(
        ((joint_t, joint_out), (grad_query, grad_query_out), (up, up_out), (gain, gain_out)), 4
    )
    for copy in reads:
        copy.start()
    reads[0].wait()
    for part in range(4):
        rows = joint[part].reshape(128, PADDED)
        joint_t[:, part * 128:(part + 1) * 128] = rows.astype(F32).T[:JOINT, :].astype(BF16)
    writes[0].start()
    for read, write in zip(reads[1:], writes[1:]):
        read.wait()
        write.start()
    for copy in writes:
        copy.wait()


def hbm_spec():
    return pl.BlockSpec(memory_space=pltpu.HBM)


def per_device(latent_with_rope, latent_norm_weight, expand_weight, queries, grad_output):
    width = expand_weight.shape[1]
    sem = pltpu.SemaphoreType.DMA
    joint_shape = (4, 2, 4, CHUNK, PADDED)
    grad_query, joint, up, gain = pl.pallas_call(
        body,
        name="attention_and_sums",
        out_shape=(
            jax.ShapeDtypeStruct(queries.shape, BF16),
            jax.ShapeDtypeStruct(joint_shape, BF16),
            jax.ShapeDtypeStruct((CHUNK, width), F32),
            jax.ShapeDtypeStruct((1, LATENT), F32),
        ),
        in_specs=[hbm_spec()] * 5,
        out_specs=(hbm_spec(),) * 4,
        scratch_shapes=[
            pltpu.VMEM((JOINT, SEQ), BF16),
            pltpu.VMEM((1, LATENT), F32),
            pltpu.VMEM(expand_weight.shape, BF16),
            pltpu.VMEM(queries.shape, BF16),
            pltpu.VMEM(grad_output.shape, BF16),
            sem((5,)),
            pltpu.VMEM(queries.shape, BF16),
            pltpu.VMEM(joint_shape, BF16),
            pltpu.VMEM((CHUNK, width), F32),
            pltpu.VMEM((1, LATENT), F32),
            sem((4,)),
            pltpu.VMEM((SEQ, LATENT), F32),
            pltpu.VMEM((SEQ, 128), F32),
            pltpu.VMEM((SEQ, LATENT), BF16),
            pltpu.VMEM((LATENT, SEQ), BF16),
            pltpu.VMEM((SEQ, 128), F32),
            pltpu.VMEM((SEQ, 128), F32),
            pltpu.VMEM((SEQ, width), BF16),
            pltpu.VMEM((SEQ, 256), BF16),
            pltpu.VMEM((SEQ, VALUE), BF16),
            pltpu.VMEM((SEQ, SEQ), BF16),
            pltpu.VMEM((SEQ, SEQ), BF16),
            pltpu.VMEM(joint_shape, BF16),
            pltpu.VMEM((8, 128), F32),
            pltpu.VMEM((16, 2, CHUNK, width), BF16),
            pltpu.VMEM((4, 4, CHUNK, PADDED), BF16),
            pltpu.VMEM((4, 4, CHUNK, PADDED), BF16),
            pltpu.VMEM((3, 4, CHUNK, PADDED), BF16),
            pltpu.VMEM((4, CHUNK, PADDED), BF16),
            pltpu.VMEM((3, CHUNK, PADDED), BF16),
            pltpu.VMEM((16, CHUNK, width), BF16),
            pltpu.VMEM((16, CHUNK, width), BF16),
            pltpu.VMEM((3, 4, CHUNK, width), BF16),
            pltpu.VMEM((4, CHUNK, width), BF16),
            pltpu.VMEM((3, CHUNK, width), BF16),
            pltpu.VMEM((2, 8, 128), F32),
            pltpu.VMEM((2, 8, 128), F32),
            pltpu.VMEM((4, 8, 128), F32),
            pltpu.VMEM((4, 8, 128), F32),
            pltpu.VMEM((4, 8, 128), F32),
            pltpu.VMEM((4, 8, 128), F32),
            sem((2, 4, 4)),
            sem((2, 3, 4)),
            sem((2, 3)),
            sem((2, 4)),
            sem((2, 3)),
            sem((2, 3)),
            sem((2, 3)),
            sem((2, 3, 4)),
            sem((2, 4, 4)),
            sem((2, 2)),
            sem((2, 4, 3)),
        ],
        compiler_params=pltpu.CompilerParams(
            collective_id=0, has_side_effects=True, vmem_limit_bytes=58 * 2**20
        ),
    )(
        latent_with_rope.T,
        latent_norm_weight.reshape(1, LATENT),
        expand_weight,
        queries,
        grad_output,
    )
    grad_queries, joint_t, grad_up_weight, gain = pl.pallas_call(
        write_body,
        name="write",
        out_shape=(
            jax.ShapeDtypeStruct(queries.shape, BF16),
            jax.ShapeDtypeStruct((JOINT, SEQ), BF16),
            jax.ShapeDtypeStruct((CHUNK, width), F32),
            jax.ShapeDtypeStruct((1, LATENT), F32),
        ),
        in_specs=[hbm_spec()] * 4,
        out_specs=(hbm_spec(),) * 4,
        scratch_shapes=[
            pltpu.VMEM(queries.shape, BF16),
            pltpu.VMEM(joint_shape, BF16),
            pltpu.VMEM((CHUNK, width), F32),
            pltpu.VMEM((1, LATENT), F32),
            pltpu.VMEM((JOINT, SEQ), BF16),
            sem((8,)),
        ],
        compiler_params=pltpu.CompilerParams(vmem_limit_bytes=58 * 2**20),
    )(grad_query, joint, up, gain)
    return grad_queries, joint_t.T, grad_up_weight, gain.reshape(LATENT)


def solution(mesh):
    assert mesh.shape["dp"] == NX * NY * NCORE and mesh.shape["tensor"] == NZ * NLO
    placed = (P("dp", None), P(), P(None, "tensor"), P("dp", "tensor"), P("dp", "tensor"))
    return jax.shard_map(
        per_device,
        mesh=mesh,
        in_specs=placed,
        out_specs=(P("dp", "tensor"), P("dp", None), P("dp", "tensor"), P()),
        check_vma=False,
    )
```

time: 76.3 us -> 72.6 us (0.952)
  the two profiles are of different devices: /device:TPU:4 before, /device:TPU:36 now
where the time goes in v2:
time: 72.6 us; the launch traced here: 72.4 us
  Pallas kernels  71.8 us (99%)
    pallas_call x1, Pallas kernels, per_device(): pl.pallas_call(body, name='attention_and_sums', out_shape=(jax.ShapeDtype...  69.3 us
    pallas_call x1, Pallas kernels, per_device(): pl.pallas_call(write_body, name='write', out_shape=(jax.ShapeDtypeStruct(...  2.48 us

profile of v2, /device:TPU:36, one launch (start us, length us, event | category | flops | bytes accessed | tf_op | source)
XLA Modules:
  0.0 72.4 jit_solution(736443792339017113)
XLA Ops:
  0.6 69.3 %attention_and_sums.1 = (bf16[512,768]{1,0:T(8,128)(2,1)}, bf16[4,2,4,16,640]{4,3,2,1,0:T(8,128)(2,1)}, f32[16,1024]{1,0:T(8,128)}, f32[1,512]{1,0:T(1,128)}) custom-call(bf16[576,512]{1,0:T(8,128)(2,1)} %bitcast.4, f32[1,512]{1,0:T(1,128)} %bitcast.5, bf16[512,1024]{1,0:T(8,128)(2,1)} %expand_hbm.1, bf16[512,768]{1,0:T(8,128)(2,1)} %query_hbm.1, ...), custom_call_target="tpu_custom_call" | custom-call | tf_op jit(solution)/shard_map/attention_and_sums/pallas_call | solution.py:441
  70.0 2.5 %write.1 = (bf16[512,768]{1,0:T(8,128)(2,1)}, bf16[576,512]{1,0:T(8,128)(2,1)}, f32[16,1024]{1,0:T(8,128)}, f32[1,512]{1,0:T(1,128)}) custom-call(bf16[512,768]{1,0:T(8,128)(2,1)} %get-tuple-element.12.grad_query_in, bf16[4,2,4,16,640]{4,3,2,1,0:T(8,128)(2,1)} %get-tuple-element.13.joint_in, f32[16,1024]{1,0:T(8,128)} %get-tuple-element.14.up_in, ...), custom_call_target="tpu_custom_call" | custom-call | tf_op jit(solution)/shard_map/write/pallas_call | solution.py:516

commit v3 on v2

--- a/solution.py
+++ b/solution.py
@@ -155,27 +155,28 @@
          lat, weight, expand, query, grad_out, load_sem, grad_query, joint, up, gain_out, save_sem,
          unit, inverse, normed, normed_t, rope_pad, rope_sum, grad_up, key_pad, value, probs,
          grad_scores, joint_part, gain_part, up_part,
-         lo_in, lo_sum, near_in, near_sum, far_in, core_in, core_sum, x_in, y_sum, y_in,
+         near_in, near_sum, far_in, core_in, core_sum, x_in, y_sum, y_in,
          gain_lo, gain_core, gain_far, gain_near, gain_x, gain_y,
-         lo_sem, near_sem, far_sem, core_sem, x_sem, y_sem, out_far_sem, out_near_sem,
-         out_lo_sem, gain_pair_sem, gain_quad_sem):
+         near_sem, far_sem, core_sem, x_sem, y_sem, out_far_sem, out_near_sem,
+         gain_pair_sem, gain_quad_sem):
     d, t = lax.axis_index("dp"), lax.axis_index("tensor")
     core, y, x = d % 2, (d // 2) % 4, d // 8
     lo, z = t % 2, t // 2
     quarter, phase = z // 4, z % 4
 
-    def z_plus(step):
-        return (d, ((z + step + NZ) % NZ) * 2 + lo)
+    def z_plus(step, side=0):
+        return (d, ((z + step + NZ) % NZ) * 2 + (1 - lo if side else lo))
 
     lo_peer = (d, t + 1 - 2 * lo)
     core_peer = (d + 1 - 2 * core, t)
     x_peers = [((((x + j) % 4) * 4 + y) * 2 + core, t) for j in (1, 2, 3)]
     y_peers = [((x * 4 + (y + j) % 4) * 2 + core, t) for j in (1, 2, 3)]
     far_peers = [z_plus(4 * j) for j in (1, 2, 3)]
-    near_peers = {s: z_plus(s) for s in (1, -1, 2, -2)}
+    near_peers = {(s, side): z_plus(s, side) for s in (1, -1, 2, -2) for side in (0, 1)}
+    near_peers[0, 1] = lo_peer
 
     barrier = pltpu.get_barrier_semaphore()
-    peers = far_peers + [lo_peer, core_peer] + x_peers + y_peers + list(near_peers.values())
+    peers = far_peers + [core_peer] + x_peers + y_peers + list(near_peers.values())
     for peer in peers:
         pl.semaphore_signal(barrier, inc=1, device_id=peer, device_id_type=MESH)
 
@@ -230,56 +231,47 @@
         return (slots[0] + slots[1]) + (slots[2] + slots[3])
 
     order = (2, 1, 3, 0)
-    deltas = (0, 1, -1, 2)
-    slot_of = {1: 0, -1: 1, 2: 2}
+    slot_of = {(1, 0): 0, (-1, 0): 1, (2, 0): 2, (0, 1): 3, (1, 1): 4, (-1, 1): 5, (2, 1): 6}
 
     def collected(step, delta):
         holder = quarter if delta in (0, 2) else ((z + delta + NZ) % NZ) // 4
         return (holder + step) % 4, (phase + delta + 4) % 4
 
-    def two_away(a):
-        return 2 - 4 * (a // 2)
+    def near_peer(delta, side, a):
+        return z_plus(2 - 4 * (a // 2), side) if delta == 2 else near_peers[delta, side]
 
     gain_pair_send(gain_part[...], gain_lo, 0, lo, lo_peer)
     for step in order:
-        for delta in deltas:
+        for (delta, side), slot in reversed(slot_of.items()):
             a, k = collected(step, delta)
-            send(joint_part.at[a, 1 - lo, k], lo_in.at[a, k], lo_sem, (a, k), (a, k), lo_peer)
+            send(joint_part.at[a, 1 - lo if side else lo, k], near_in.at[slot, a], near_sem,
+                 (slot, a), (slot, a), near_peer(delta, side, a))
 
     up_gradient(normed_t, grad_up, up_part)
     for i in range(4):
         send(up_part.at[pl.ds(4 * i, 4), 1 - core], core_in.at[pl.ds(4 * i, 4)], core_sem,
              (i,), (i,), core_peer)
 
-    def lo_step(step):
-        for delta in deltas:
-            a, k = collected(step, delta)
-            arrive(lo_in.at[a, k], lo_sem, (a, k), lo_peer)
-            lo_sum[a, k] = (
-                joint_part[a, lo, k].astype(F32) + lo_in[a, k].astype(F32)
-            ).astype(BF16)
-            if delta:
-                slot = slot_of[delta]
-                peer = z_plus(two_away(a)) if delta == 2 else near_peers[delta]
-                send(lo_sum.at[a, k], near_in.at[slot, a], near_sem, (slot, a), (slot, a), peer)
-
     def near_step(step):
         a = (quarter + step) % 4
-        for delta in deltas[1:]:
-            slot = slot_of[delta]
-            arrive(near_in.at[slot, a], near_sem, (slot, a), near_peers[-delta])
+        for (delta, side), slot in slot_of.items():
+            arrive(near_in.at[slot, a], near_sem, (slot, a), near_peers[-delta, side])
         near_sum[a] = (
-            (lo_sum[a, phase].astype(F32) + near_in[0, a].astype(F32))
-            + (near_in[1, a].astype(F32) + near_in[2, a].astype(F32))
+            (
+                (joint_part[a, lo, phase].astype(F32) + near_in[0, a].astype(F32))
+                + (near_in[1, a].astype(F32) + near_in[2, a].astype(F32))
+            )
+            + (
+                (near_in[3, a].astype(F32) + near_in[4, a].astype(F32))
+                + (near_in[5, a].astype(F32) + near_in[6, a].astype(F32))
+            )
         ).astype(BF16)
         if step:
             send(near_sum.at[a], far_in.at[step - 1], far_sem, (step - 1,), (step - 1,),
                  far_peers[step - 1])
 
-    lo_step(order[0])
     gain_value = gain_pair_sum(gain_lo, 0, lo, lo_peer)
     gain_pair_send(gain_value, gain_core, 1, core, core_peer)
-    lo_step(order[1])
     gain_value = gain_pair_sum(gain_core, 1, core, core_peer)
     gain_quad_send(gain_value, gain_far, 0, quarter, far_peers)
 
@@ -293,14 +285,10 @@
         if j:
             send(core_sum.at[rows], x_in.at[j - 1], x_sem, (j - 1,), (j - 1,), x_peers[j - 1])
 
-    near_step(order[0])
-    lo_step(order[2])
-    near_step(order[1])
-    lo_step(order[3])
-    near_step(order[2])
-    near_step(order[3])
+    for step in order:
+        near_step(step)
     gain_value = gain_quad_sum(gain_far, 0, quarter, (1, 2, 3), far_peers[::-1])
-    gain_near_peers = [near_peers[1], near_peers[-1], near_peers[2]]
+    gain_near_peers = [near_peers[1, 0], near_peers[-1, 0], near_peers[2, 0]]
     gain_quad_send(gain_value, gain_near, 1, phase, gain_near_peers)
 
     first = pl.multiple_of(quarter * 128 + lo * 64 + phase * CHUNK, CHUNK)
@@ -317,16 +305,6 @@
     )
     joint[quarter, lo, phase, :, :LATENT] = grad_latent.astype(BF16)
     joint[quarter, lo, phase, :, LATENT:] = total[:, LATENT:].astype(BF16)
-
-    def to_lo(a, k):
-        chunk = joint.at[a, lo, k]
-        return pltpu.make_async_remote_copy(
-            src_ref=chunk, dst_ref=chunk, send_sem=out_lo_sem.at[0, a, k],
-            recv_sem=out_lo_sem.at[1, a, k], device_id=lo_peer, device_id_type=MESH,
-        )
-
-    def pass_on(a, k):
-        to_lo(a, k).start()
 
     def spread(step):
         a = (quarter + 4 - step) % 4
@@ -336,28 +314,12 @@
         else:
             for j in (2, 1, 3):
                 send(chunk, chunk, out_far_sem, (j - 1,), (j - 1,), far_peers[j - 1])
-        for slot, peer in ((2, z_plus(two_away(a))), (0, near_peers[1]), (1, near_peers[-1])):
-            send(chunk, chunk, out_near_sem, (slot, a), (slot, a), peer)
-        pass_on(a, phase)
-
-    def from_near(step):
-        for delta in (1, -1, 2, -2):
-            a = (((z - delta + NZ) % NZ) // 4 + 4 - step) % 4
-            k = (phase - delta + 4) % 4
-            slot = 2 if abs(delta) == 2 else slot_of[delta]
-
-            def relay(a=a, k=k, slot=slot, delta=delta):
-                arrive(joint.at[a, lo, k], out_near_sem, (slot, a), near_peers[-delta])
-                pass_on(a, k)
-
-            if slot < 2:
-                relay()
-            else:
-                pl.when(a < 2 if delta == 2 else a >= 2)(relay)
+        for (delta, side), slot in reversed(slot_of.items()):
+            send(chunk, chunk, out_near_sem, (slot, a), (slot, a), near_peer(delta, side, a))
 
     spread(0)
     gain_value = gain_quad_sum(
-        gain_near, 1, phase, (1, 3, 2), [near_peers[-1], near_peers[1], near_peers[-2]]
+        gain_near, 1, phase, (1, 3, 2), [near_peers[-1, 0], near_peers[1, 0], near_peers[-2, 0]]
     )
     gain_quad_send(gain_value, gain_x, 2, x, x_peers)
     for j in (1, 3, 2):
@@ -368,13 +330,10 @@
     ).astype(BF16)
     for j in (2, 1, 3):
         send(y_sum.at[(y + j) % 4], y_in.at[j - 1], y_sem, (j - 1,), (j - 1,), y_peers[j - 1])
-    from_near(0)
     gain_value = gain_quad_sum(gain_x, 2, x, (1, 2, 3), x_peers[::-1])
     gain_quad_send(gain_value, gain_y, 3, y, y_peers)
     spread(1)
     spread(3)
-    from_near(1)
-    from_near(3)
     spread(2)
     for j in (1, 3, 2):
         arrive(y_in.at[j - 1], y_sem, (j - 1,), y_peers[3 - j])
@@ -383,20 +342,17 @@
     )
     saves.append(pltpu.make_async_copy(up, up_hbm, save_sem.at[1]))
     saves[-1].start()
-    from_near(2)
     gain_value = gain_quad_sum(gain_y, 3, y, (1, 2, 3), y_peers[::-1])
     for piece in range(4):
         gain_out[:, piece * 128:(piece + 1) * 128] = gain_value[piece:piece + 1, :]
     saves.append(pltpu.make_async_copy(gain_out, gain_hbm, save_sem.at[2]))
     saves[-1].start()
-    for a in range(4):
-        for k in range(4):
-            arrive(joint.at[a, 1 - lo, k], out_lo_sem, (a, k), lo_peer)
+    for (delta, side), slot in slot_of.items():
+        for a in range(4):
+            chunk = joint.at[a, 1 - lo if side else lo, (phase - delta + 4) % 4]
+            arrive(chunk, out_near_sem, (slot, a), near_peers[-delta, side])
     saves.append(pltpu.make_async_copy(joint, joint_hbm, save_sem.at[3]))
     saves[-1].start()
-    for a in range(4):
-        for k in range(4):
-            to_lo(a, k).wait_send()
     for copy in started:
         copy.wait_send()
     for save in saves:
@@ -475,9 +431,7 @@
             pltpu.VMEM(joint_shape, BF16),
             pltpu.VMEM((8, 128), F32),
             pltpu.VMEM((16, 2, CHUNK, width), BF16),
-            pltpu.VMEM((4, 4, CHUNK, PADDED), BF16),
-            pltpu.VMEM((4, 4, CHUNK, PADDED), BF16),
-            pltpu.VMEM((3, 4, CHUNK, PADDED), BF16),
+            pltpu.VMEM((7, 4, CHUNK, PADDED), BF16),
             pltpu.VMEM((4, CHUNK, PADDED), BF16),
             pltpu.VMEM((3, CHUNK, PADDED), BF16),
             pltpu.VMEM((16, CHUNK, width), BF16),
@@ -491,15 +445,13 @@
             pltpu.VMEM((4, 8, 128), F32),
             pltpu.VMEM((4, 8, 128), F32),
             pltpu.VMEM((4, 8, 128), F32),
-            sem((2, 4, 4)),
-            sem((2, 3, 4)),
+            sem((2, 7, 4)),
             sem((2, 3)),
             sem((2, 4)),
             sem((2, 3)),
             sem((2, 3)),
             sem((2, 3)),
-            sem((2, 3, 4)),
-            sem((2, 4, 4)),
+            sem((2, 7, 4)),
             sem((2, 2)),
             sem((2, 4, 3)),
         ],

time: 72.6 us -> 58.2 us (0.80)
  the two profiles are of different devices: /device:TPU:36 before, /device:TPU:64 now
where the time goes in v3:
time: 58.2 us; the launch traced here: 58 us
  Pallas kernels  57.3 us (98%)
  between operations  0.64 us (1%)
    pallas_call x1, Pallas kernels, per_device(): pl.pallas_call(body, name='attention_and_sums', out_shape=(jax.ShapeDtype...  54.9 us
    pallas_call x1, Pallas kernels, per_device(): pl.pallas_call(write_body, name='write', out_shape=(jax.ShapeDtypeStruct(...  2.48 us

profile of v3, /device:TPU:64, one launch (start us, length us, event | category | flops | bytes accessed | tf_op | source)
XLA Modules:
  0.0 58.0 jit_solution(12499314732485268682)
XLA Ops:
  0.6 54.9 %attention_and_sums.1 = (bf16[512,768]{1,0:T(8,128)(2,1)}, bf16[4,2,4,16,640]{4,3,2,1,0:T(8,128)(2,1)}, f32[16,1024]{1,0:T(8,128)}, f32[1,512]{1,0:T(1,128)}) custom-call(bf16[576,512]{1,0:T(8,128)(2,1)} %bitcast.4, f32[1,512]{1,0:T(1,128)} %bitcast.5, bf16[512,1024]{1,0:T(8,128)(2,1)} %expand_hbm.1, bf16[512,768]{1,0:T(8,128)(2,1)} %query_hbm.1, ...), custom_call_target="tpu_custom_call" | custom-call | tf_op jit(solution)/shard_map/attention_and_sums/pallas_call | solution.py:397
  55.5 2.5 %write.1 = (bf16[512,768]{1,0:T(8,128)(2,1)}, bf16[576,512]{1,0:T(8,128)(2,1)}, f32[16,1024]{1,0:T(8,128)}, f32[1,512]{1,0:T(1,128)}) custom-call(bf16[512,768]{1,0:T(8,128)(2,1)} %get-tuple-element.12.grad_query_in, bf16[4,2,4,16,640]{4,3,2,1,0:T(8,128)(2,1)} %get-tuple-element.13.joint_in, f32[16,1024]{1,0:T(8,128)} %get-tuple-element.14.up_in, ...), custom_call_target="tpu_custom_call" | custom-call | tf_op jit(solution)/shard_map/write/pallas_call | solution.py:468

commit v4 on v3

--- a/solution.py
+++ b/solution.py
@@ -13,7 +13,7 @@
 VALUE = 128
 LATENT = 512
 JOINT = LATENT + ROPE
-PADDED = LATENT + 128
+PADDED = LATENT + ROPE
 SEQ = 512
 HALF = SEQ // 2
 CHUNK = 16
@@ -132,8 +132,8 @@
         joint_part[part, :, :, :, :LATENT] = grad_normed.astype(BF16).reshape(
             2, 4, CHUNK, LATENT
         )
-        joint_part[part, :, :, :, LATENT:] = rope_sum[rows, :].astype(BF16).reshape(
-            2, 4, CHUNK, 128
+        joint_part[part, :, :, :, LATENT:] = rope_sum[rows, :ROPE].astype(BF16).reshape(
+            2, 4, CHUNK, ROPE
         )
     gain_part[...] = jnp.zeros_like(gain_part)
     for piece in range(4):
@@ -330,10 +330,10 @@
     ).astype(BF16)
     for j in (2, 1, 3):
         send(y_sum.at[(y + j) % 4], y_in.at[j - 1], y_sem, (j - 1,), (j - 1,), y_peers[j - 1])
+    spread(1)
+    spread(3)
     gain_value = gain_quad_sum(gain_x, 2, x, (1, 2, 3), x_peers[::-1])
     gain_quad_send(gain_value, gain_y, 3, y, y_peers)
-    spread(1)
-    spread(3)
     spread(2)
     for j in (1, 3, 2):
         arrive(y_in.at[j - 1], y_sem, (j - 1,), y_peers[3 - j])

time: 58.2 us -> 59.1 us (1.015)
  the two profiles are of different devices: /device:TPU:64 before, /device:TPU:2 now
where the time goes in v4:
time: 59.1 us; the launch traced here: 58.9 us
  Pallas kernels  58.2 us (98%)
  between operations  0.64 us (1%)
    pallas_call x1, Pallas kernels, per_device(): pl.pallas_call(body, name='attention_and_sums', out_shape=(jax.ShapeDtype...  55.7 us
    pallas_call x1, Pallas kernels, per_device(): pl.pallas_call(write_body, name='write', out_shape=(jax.ShapeDtypeStruct(...  2.48 us

profile of v4, /device:TPU:2, one launch (start us, length us, event | category | flops | bytes accessed | tf_op | source)
XLA Modules:
  0.0 58.9 jit_solution(49179584313692606)
XLA Ops:
  0.6 55.7 %attention_and_sums.1 = (bf16[512,768]{1,0:T(8,128)(2,1)}, bf16[4,2,4,16,576]{4,3,2,1,0:T(8,128)(2,1)}, f32[16,1024]{1,0:T(8,128)}, f32[1,512]{1,0:T(1,128)}) custom-call(bf16[576,512]{1,0:T(8,128)(2,1)} %bitcast.4, f32[1,512]{1,0:T(1,128)} %bitcast.5, bf16[512,1024]{1,0:T(8,128)(2,1)} %expand_hbm.1, bf16[512,768]{1,0:T(8,128)(2,1)} %query_hbm.1, ...), custom_call_target="tpu_custom_call" | custom-call | tf_op jit(solution)/shard_map/attention_and_sums/pallas_call | solution.py:397
  56.4 2.5 %write.1 = (bf16[512,768]{1,0:T(8,128)(2,1)}, bf16[576,512]{1,0:T(8,128)(2,1)}, f32[16,1024]{1,0:T(8,128)}, f32[1,512]{1,0:T(1,128)}) custom-call(bf16[512,768]{1,0:T(8,128)(2,1)} %get-tuple-element.12.grad_query_in, bf16[4,2,4,16,576]{4,3,2,1,0:T(8,128)(2,1)} %get-tuple-element.13.joint_in, f32[16,1024]{1,0:T(8,128)} %get-tuple-element.14.up_in, ...), custom_call_target="tpu_custom_call" | custom-call | tf_op jit(solution)/shard_map/write/pallas_call | solution.py:468
